TPU v7x, 256 devices: a whole 4x4x8 slice. The times are simulated.
256 devices in a mesh: seq: 128 (over z, y, x), state: 2 (over core).
Axes of the slice: x: 4, y: 4, z: 8, core: 2. Of those that a mesh axis runs over, the one named last changes fastest.
Arguments:
- inputs: bfloat16 [4, 16384, 2048], P(None, 'seq'), may hold values from -6 to 6
- in_proj: bfloat16 [2048, 2, 1024], P(None, None, 'state'), may hold values from -0.125 to 0.125
- decay_rate: float32 [1024], P('state'), may hold values from 1.2207031e-05 to 0.04
- frequency: float32 [1024], P('state'), may hold values from -3.140625 to 3.140625
- readout: bfloat16 [2, 1024, 2048], P(None, 'state'), may hold values from -0.125 to 0.125
- skip_gain: float32 [2048], P('state'), may hold values from 0.5 to 1.5
Outputs:
- outputs: bfloat16 [4, 16384, 2048], P(None, 'seq', 'state')
All inputs are finite; a program needn't handle non-finite values.
Results may differ from a plain program's by a relative error of at most 0.004.
Values may be sent and summed in bfloat16 or wider, within the bound.
A program may use at most 128 MiB of HBM per device.

v0:
```python
import functools

import jax
import jax.numpy as jnp
from jax import lax
from jax.experimental import pallas as pl
from jax.experimental.pallas import tpu as pltpu
from jax.sharding import PartitionSpec as P

F32 = jnp.float32
BF16 = jnp.bfloat16
MESH_ID = pl.DeviceIdType.MESH

SEQS = 4
STEPS = 128
ROWS = SEQS * STEPS
WIDTH = 2048
POLES = 512
GROUPS = 2
GP = POLES // GROUPS
SUB = 16
CHUNKS = ROWS // SUB
KC = 512
KN = WIDTH // KC
COLS = 1024
LANES = 128
GT = GP // LANES
OT = COLS // LANES
PLANE = 16
DEPTH = 8
PLANE_ORDER = sorted(range(1, PLANE), key=lambda d: -(min(d % 4, 4 - d % 4) + min(d // 4, 4 - d // 4)))
DEPTH_ORDER = sorted(range(1, DEPTH), key=lambda d: -min(d, DEPTH - d))


def cmul(ar, ai, br, bi):
    return ar * br - ai * bi, ar * bi + ai * br


def kernel(
    x_hbm, w_hbm, dec_ref, frq_ref, r_hbm, skip_ref, out_hbm,
    x_v, w_raw, w_v, r_own, r_sib, drive, ends, excl, packed, packed_sib, acc, out_v,
    plane_buf, depth_buf, lam_tab, pow_tab, dep_tab,
    x_sem, w_sem, r_sem, o_sem, rs_send, rs_recv, pl_send, pl_recv, dp_send, dp_recv, pk_send, pk_recv,
):
    me, core = lax.axis_index("seq"), lax.axis_index("state")
    spot, deep = lax.rem(me, PLANE), lax.div(me, PLANE)
    px, py = lax.rem(spot, 4), lax.div(spot, 4)

    def plane_peer(d):
        spot_to = lax.rem(py + d // 4, 4) * 4 + lax.rem(px + d % 4, 4)
        return (deep * PLANE + spot_to, core), spot_to

    def plane_from(d):
        return lax.rem(py + 4 - d // 4, 4) * 4 + lax.rem(px + 4 - d % 4, 4)

    def depth_peer(d):
        return (lax.rem(deep + d, DEPTH) * PLANE + spot, core)

    sibling = (me, 1 - core)

    x_cps, w_cps = [], [[] for _ in range(GROUPS)]
    for k in range(KN):
        cp = pltpu.make_async_copy(x_hbm.at[:, pl.ds(KC * k, KC)], x_v.at[:, pl.ds(KC * k, KC)], x_sem.at[k])
        cp.start()
        x_cps.append(cp)
        cp = pltpu.make_async_copy(w_hbm.at[pl.ds(KC * k, KC), :, pl.ds(0, GP)], w_raw.at[0, k], w_sem.at[0, k])
        cp.start()
        w_cps[0].append(cp)
    for g in range(1, GROUPS):
        for k in range(KN):
            cp = pltpu.make_async_copy(w_hbm.at[pl.ds(KC * k, KC), :, pl.ds(GP * g, GP)], w_raw.at[g, k], w_sem.at[g, k])
            cp.start()
            w_cps[g].append(cp)
    my_cols = pl.multiple_of(core * COLS, COLS)
    sib_cols = pl.multiple_of((1 - core) * COLS, COLS)
    r_cps = []
    for g in range(GROUPS):
        for c in range(2):
            cp = pltpu.make_async_copy(
                r_hbm.at[c, pl.ds(GP * g, GP), pl.ds(my_cols, COLS)], r_own.at[g, pl.ds(GP * c, GP)], r_sem.at[g, c]
            )
            cp.start()
            r_cps.append(cp)

    barrier = pltpu.get_barrier_semaphore()
    for d in DEPTH_ORDER:
        pl.semaphore_signal(barrier, inc=1, device_id=depth_peer(d), device_id_type=MESH_ID)
    for d in PLANE_ORDER:
        pl.semaphore_signal(barrier, inc=1, device_id=plane_peer(d)[0], device_id_type=MESH_ID)
    pl.semaphore_signal(barrier, inc=1, device_id=sibling, device_id_type=MESH_ID)

    dec, frq = dec_ref[...], frq_ref[...]
    mod = jnp.exp(-dec)
    sq = dec * dec
    sinh = dec * (1.0 + sq / 6.0 * (1.0 + sq / 20.0 * (1.0 + sq / 42.0 * (1.0 + sq / 72.0))))
    gam = jnp.sqrt(2.0 * mod * sinh)
    base = (mod * jnp.cos(frq), mod * jnp.sin(frq))
    powers = [None, base]
    for n in range(2, SUB + 1):
        half = powers[n // 2]
        full = cmul(*half, *half)
        powers.append(cmul(*full, *base) if n % 2 else full)
    for n in range(SUB):
        pow_tab[0, pl.ds(n, 1), :] = powers[n + 1][0]
        pow_tab[1, pl.ds(n, 1), :] = powers[n + 1][1]
    one = (jnp.ones_like(dec), jnp.zeros_like(dec))
    subs = [one, powers[SUB]]
    for n in range(2, 9):
        subs.append(cmul(*subs[n // 2], *subs[n - n // 2]))
    sub_re = jnp.concatenate([p[0] for p in subs[:8]], axis=0)
    sub_im = jnp.concatenate([p[1] for p in subs[:8]], axis=0)
    lams = [one, subs[8]]
    for n in range(2, PLANE + 1):
        lams.append(cmul(*lams[n // 2], *lams[n - n // 2]))
    for n in range(PLANE):
        lam_tab[0, pl.ds(n, 1), :] = lams[n][0]
        lam_tab[1, pl.ds(n, 1), :] = lams[n][1]
    lead = lams[PLANE]
    here = (lam_tab[0, pl.ds(spot, 1), :], lam_tab[1, pl.ds(spot, 1), :])
    weight = (jnp.zeros_like(dec), jnp.zeros_like(dec))
    for n in range(DEPTH - 1, -1, -1):
        longer = cmul(*weight, *lead)
        first = deep - 1 == n
        weight = tuple(jnp.where(first, h, w) for h, w in zip(here, longer))
        dep_tab[0, pl.ds(n, 1), :] = weight[0]
        dep_tab[1, pl.ds(n, 1), :] = weight[1]

    step_of = lax.rem(lax.broadcasted_iota(jnp.int32, (CHUNKS, GP), 0), 8)
    sign = jnp.where(lax.broadcasted_iota(jnp.int32, (8, GP), 0) < 4, -1.0, 1.0)

    def weighted(parts, tab, order, lanes):
        along = jnp.zeros((8, GP), F32)
        across = jnp.zeros((8, GP), F32)
        for n, part in enumerate(parts):
            along = along + tab[0, pl.ds(order[n], 1), lanes] * part
            across = across + tab[1, pl.ds(order[n], 1), lanes] * part
        return along + sign * pltpu.roll(across, 4, 0)

    plane_cps, depth_cps, pack_cps, rs_cps = [[] for _ in range(GROUPS)], [[] for _ in range(GROUPS)], [], []

    for k in range(KN):
        x_cps[k].wait()
    for g in range(GROUPS):
        lanes = pl.ds(GP * g, GP)
        for k in range(KN):
            w_cps[g][k].wait()

            def turn(n, carry):
                for u in range(4):
                    at = pl.multiple_of(n * 64 + u * 16, 16)
                    both = jnp.swapaxes(w_raw[g, k, pl.ds(at, 16)], 0, 1)
                    w_v[pl.ds(KC * k + at, 16), pl.ds(0, GP)] = both[0]
                    w_v[pl.ds(KC * k + at, 16), pl.ds(GP, GP)] = both[1]
                return carry

            lax.fori_loop(0, KC // 64, turn, 0)
        driven = jnp.dot(x_v[...], w_v[...], preferred_element_type=F32)
        for t in range(2 * GT):
            drive[g, t] = driven[:, LANES * t : LANES * (t + 1)]

        lr, li = base[0][:, GP * g : GP * (g + 1)], base[1][:, GP * g : GP * (g + 1)]
        gg = gam[:, GP * g : GP * (g + 1)]
        sr = jnp.zeros((CHUNKS, GP), F32)
        si = jnp.zeros((CHUNKS, GP), F32)
        for i in range(SUB):
            tiles = [drive[g, t, pl.ds(i, CHUNKS, stride=SUB), :] for t in range(2 * GT)]
            nr = lr * sr - li * si + gg * jnp.concatenate(tiles[:GT], axis=1)
            ni = lr * si + li * sr + gg * jnp.concatenate(tiles[GT:], axis=1)
            sr, si = nr, ni
            ends[g, pl.ds(CHUNKS * i, CHUNKS), pl.ds(0, GP)] = sr
            ends[g, pl.ds(CHUNKS * i, CHUNKS), pl.ds(GP, GP)] = si
        for d in (1, 2, 4):
            mr = jnp.where(step_of >= d, subs[d][0][:, GP * g : GP * (g + 1)], 0.0)
            mi = jnp.where(step_of >= d, subs[d][1][:, GP * g : GP * (g + 1)], 0.0)
            tr, ti = pltpu.roll(sr, d, 0), pltpu.roll(si, d, 0)
            sr, si = sr + mr * tr - mi * ti, si + mr * ti + mi * tr
        for s in range(SEQS):
            plane_buf[g, spot, pl.ds(s, 1), :] = sr[8 * s + 7 : 8 * s + 8]
            plane_buf[g, spot, pl.ds(4 + s, 1), :] = si[8 * s + 7 : 8 * s + 8]
        excl[g, 0] = jnp.where(step_of >= 1, pltpu.roll(sr, 1, 0), 0.0)
        excl[g, 1] = jnp.where(step_of >= 1, pltpu.roll(si, 1, 0), 0.0)

        if g == 0:
            pl.semaphore_wait(barrier, DEPTH + PLANE - 1)
        for d in PLANE_ORDER:
            cp = pltpu.make_async_remote_copy(
                src_ref=plane_buf.at[g, spot], dst_ref=plane_buf.at[g, spot], send_sem=pl_send.at[g, d],
                recv_sem=pl_recv.at[g, d], device_id=plane_peer(d)[0], device_id_type=MESH_ID,
            )
            cp.start()
            plane_cps[g].append(cp)
        if g == GROUPS - 1:
            for h in range(GROUPS):
                for c in range(2):
                    cp = pltpu.make_async_remote_copy(
                        src_ref=r_hbm.at[c, pl.ds(GP * h, GP), pl.ds(sib_cols, COLS)],
                        dst_ref=r_sib.at[h, pl.ds(GP * c, GP)], send_sem=rs_send.at[h, c],
                        recv_sem=rs_recv.at[h, c], device_id=sibling, device_id_type=MESH_ID,
                    )
                    cp.start()
                    rs_cps.append(cp)

    entering = []
    for g in range(GROUPS):
        lanes = pl.ds(GP * g, GP)
        for cp in plane_cps[g]:
            cp.wait_recv()
        parts = [plane_buf[g, n] for n in range(PLANE)]
        depth_buf[g, deep] = weighted(parts, lam_tab, [PLANE - 1 - n for n in range(PLANE)], lanes)
        for d in DEPTH_ORDER:
            cp = pltpu.make_async_remote_copy(
                src_ref=depth_buf.at[g, deep], dst_ref=depth_buf.at[g, deep], send_sem=dp_send.at[g, d],
                recv_sem=dp_recv.at[g, d], device_id=depth_peer(d), device_id_type=MESH_ID,
            )
            cp.start()
            depth_cps[g].append(cp)
        lam_re, lam_im = lam_tab[0, pl.ds(1, 1), lanes], lam_tab[1, pl.ds(1, 1), lanes] * sign
        before = jnp.zeros((8, GP), F32)
        for n in range(PLANE - 1):
            longer = lam_re * before + lam_im * pltpu.roll(before, 4, 0) + parts[n]
            before = jnp.where(n < spot, longer, before)
        entering.append(before)
    for cp in r_cps:
        cp.wait()
    for cp in rs_cps:
        cp.wait_recv()

    skip = skip_ref[...]
    for g in range(GROUPS):
        lanes = pl.ds(GP * g, GP)
        for cp in depth_cps[g]:
            cp.wait_recv()
        come = entering[g] + weighted([depth_buf[g, n] for n in range(DEPTH)], dep_tab, list(range(DEPTH)), lanes)
        cr = jnp.concatenate([jnp.broadcast_to(come[s : s + 1], (8, GP)) for s in range(SEQS)], axis=0)
        ci = jnp.concatenate([jnp.broadcast_to(come[4 + s : 5 + s], (8, GP)) for s in range(SEQS)], axis=0)
        qr = jnp.concatenate([sub_re[:, GP * g : GP * (g + 1)]] * SEQS, axis=0)
        qi = jnp.concatenate([sub_im[:, GP * g : GP * (g + 1)]] * SEQS, axis=0)
        tr = excl[g, 0] + qr * cr - qi * ci
        ti = excl[g, 1] + qr * ci + qi * cr
        for i in range(SUB):
            ar, ai = pow_tab[0, pl.ds(i, 1), lanes], pow_tab[1, pl.ds(i, 1), lanes]
            rows = pl.ds(CHUNKS * i, CHUNKS)
            packed[g, rows, pl.ds(0, GP)] = (ends[g, rows, pl.ds(0, GP)] + ar * tr - ai * ti).astype(BF16)
            packed[g, rows, pl.ds(GP, GP)] = (ends[g, rows, pl.ds(GP, GP)] + ar * ti + ai * tr).astype(BF16)
        cp = pltpu.make_async_remote_copy(
            src_ref=packed.at[g], dst_ref=packed_sib.at[g], send_sem=pk_send.at[g], recv_sem=pk_recv.at[g],
            device_id=sibling, device_id_type=MESH_ID,
        )
        cp.start()
        pack_cps.append(cp)
        part = jnp.dot(packed[g], r_own[g], preferred_element_type=F32)
        for t in range(OT):
            tile = part[:, LANES * t : LANES * (t + 1)]
            acc[t] = tile if g == 0 else acc[t] + tile
        cp.wait_recv()
        if g < GROUPS - 1:
            part = jnp.dot(packed_sib[g], r_sib[g], preferred_element_type=F32)
            for t in range(OT):
                acc[t] += part[:, LANES * t : LANES * (t + 1)]
    out_cps = []
    last = GROUPS - 1
    CN = 256
    for c in range(COLS // CN):
        part = jnp.dot(packed_sib[last], r_sib[last, :, pl.ds(CN * c, CN)], preferred_element_type=F32)
        of_chunk = range(CN // LANES * c, CN // LANES * (c + 1))
        for n, t in enumerate(of_chunk):
            acc[t] += part[:, LANES * n : LANES * (n + 1)]
        gain = skip[:, CN * c : CN * (c + 1)]
        from_col = pl.multiple_of(core * COLS + CN * c, CN)
        for q in range(CHUNKS):
            straight = x_v[pl.ds(SUB * q, SUB), pl.ds(from_col, CN)].astype(F32) * gain
            summed = jnp.concatenate([acc[t, pl.ds(q, SUB, stride=CHUNKS), :] for t in of_chunk], axis=1)
            out_v[pl.ds(SUB * q, SUB), pl.ds(CN * c, CN)] = (summed + straight).astype(BF16)
        cp = pltpu.make_async_copy(out_v.at[:, pl.ds(CN * c, CN)], out_hbm.at[:, pl.ds(CN * c, CN)], o_sem.at[c])
        cp.start()
        out_cps.append(cp)
    for cp in out_cps:
        cp.wait()
    for g in range(GROUPS):
        for cp in plane_cps[g] + depth_cps[g]:
            cp.wait_send()
    for cp in pack_cps + rs_cps:
        cp.wait_send()


def local(inputs, in_proj, decay_rate, frequency, readout, skip_gain):
    vmem = pl.BlockSpec(memory_space=pltpu.VMEM)
    hbm = pl.BlockSpec(memory_space=pl.ANY)
    dma = pltpu.SemaphoreType.DMA
    out = pl.pallas_call(
        kernel,
        out_shape=jax.ShapeDtypeStruct((ROWS, COLS), BF16),
        in_specs=[hbm, hbm, vmem, vmem, hbm, vmem],
        out_specs=hbm,
        scratch_shapes=[
            pltpu.VMEM((ROWS, WIDTH), BF16),
            pltpu.VMEM((GROUPS, KN, KC, 2, GP), BF16),
            pltpu.VMEM((WIDTH, 2 * GP), BF16),
            pltpu.VMEM((GROUPS, 2 * GP, COLS), BF16),
            pltpu.VMEM((GROUPS, 2 * GP, COLS), BF16),
            pltpu.VMEM((GROUPS, 2 * GT, ROWS, LANES), F32),
            pltpu.VMEM((GROUPS, ROWS, 2 * GP), F32),
            pltpu.VMEM((GROUPS, 2, CHUNKS, GP), F32),
            pltpu.VMEM((GROUPS, ROWS, 2 * GP), BF16),
            pltpu.VMEM((GROUPS, ROWS, 2 * GP), BF16),
            pltpu.VMEM((OT, ROWS, LANES), F32),
            pltpu.VMEM((ROWS, COLS), BF16),
            pltpu.VMEM((GROUPS, PLANE, 8, GP), F32),
            pltpu.VMEM((GROUPS, DEPTH, 8, GP), F32),
            pltpu.VMEM((2, PLANE, POLES), F32),
            pltpu.VMEM((2, SUB, POLES), F32),
            pltpu.VMEM((2, DEPTH, POLES), F32),
            dma((KN,)),
            dma((GROUPS, KN)),
            dma((GROUPS, 2)),
            dma((4,)),
            dma((GROUPS, 2)),
            dma((GROUPS, 2)),
            dma((GROUPS, PLANE)),
            dma((GROUPS, PLANE)),
            dma((GROUPS, DEPTH)),
            dma((GROUPS, DEPTH)),
            dma((GROUPS,)),
            dma((GROUPS,)),
        ],
        compiler_params=pltpu.CompilerParams(
            collective_id=0, has_side_effects=True, vmem_limit_bytes=48 << 20
        ),
    )(
        inputs.reshape(ROWS, WIDTH), in_proj, decay_rate.reshape(1, POLES), frequency.reshape(1, POLES),
        readout, skip_gain.reshape(1, COLS),
    )
    return out.reshape(SEQS, STEPS, COLS)


def solution(mesh):
    in_specs = (
        P(None, "seq", None),
        P(None, None, "state"),
        P("state"),
        P("state"),
        P(None, "state", None),
        P("state"),
    )
    out_specs = P(None, "seq", "state")
    return jax.shard_map(local, mesh=mesh, in_specs=in_specs, out_specs=out_specs, check_vma=False)
```

profile of v0, /device:TPU:1, one launch (start us, length us, event | category | flops | bytes accessed | tf_op | source)
XLA Modules:
  0.0 35.3 jit_solution(15494030335211003204)
XLA Ops:
  0.0 0.0 copy-start
  0.0 1.6 %copy-done = bf16[4,128,2048]{2,1,0:T(8,128)(2,1)S(1)} copy-done((bf16[4,128,2048]{2,1,0:T(8,128)(2,1)S(1)}, bf16[4,128,2048]{2,1,0:T(8,128)(2,1)}, u32[]{:S(2)}) %copy-start) | copy-done | bytes 2097176
  1.6 0.0 copy-start.1
  1.6 0.7 %copy-done.1 = f32[1024]{0:T(1024)S(1)} copy-done((f32[1024]{0:T(1024)S(1)}, f32[1024]{0:T(1024)}, u32[]{:S(2)}) %copy-start.1) | copy-done | bytes 4120
  2.3 0.0 copy-start.2
  2.3 0.7 %copy-done.2 = f32[512]{0:T(512)S(1)} copy-done((f32[512]{0:T(512)S(1)}, f32[512]{0:T(512)}, u32[]{:S(2)}) %copy-start.2) | copy-done | bytes 2072
  3.0 0.0 copy-start.3
  3.0 0.7 %copy-done.3 = f32[512]{0:T(512)S(1)} copy-done((f32[512]{0:T(512)S(1)}, f32[512]{0:T(512)}, u32[]{:S(2)}) %copy-start.3) | copy-done | bytes 2072
  3.6 30.7 %shard_map.64 = bf16[512,1024]{1,0:T(8,128)(2,1)S(1)} custom-call(bf16[512,2048]{1,0:T(8,128)(2,1)S(1)} %bitcast.6, bf16[2048,2,512]{2,1,0:T(2,128)(2,1)} %w_hbm.1, f32[1,512]{1,0:T(1,128)S(1)} %bitcast.8, f32[1,512]{1,0:T(1,128)S(1)} %bitcast.9, bf16[2,512,2048]{2,1,0:T(8,128)(2,1)} %r_hbm.1, f32[1,1024]{1,0:T(1,128)S(1)} %bitcast.7), custom_call_target="tpu_custom_call" | custom-call | tf_op jit(solution)/shard_map/pallas_call | solution.py:290
  34.3 1.0 %copy.8 = bf16[4,128,1024]{2,1,0:T(8,128)(2,1)} copy(bf16[4,128,1024]{2,1,0:T(8,128)(2,1)S(1)} %bitcast.5) | data formatting | bytes 2097152
Async XLA Ops:
  0.0 1.6 %copy-start = (bf16[4,128,2048]{2,1,0:T(8,128)(2,1)S(1)}, bf16[4,128,2048]{2,1,0:T(8,128)(2,1)}, u32[]{:S(2)}) copy-start(bf16[4,128,2048]{2,1,0:T(8,128)(2,1)} %param.6) | copy-start | bytes 6291460
  1.6 0.7 %copy-start.1 = (f32[1024]{0:T(1024)S(1)}, f32[1024]{0:T(1024)}, u32[]{:S(2)}) copy-start(f32[1024]{0:T(1024)} %param.11) | copy-start | bytes 12292
  2.3 0.7 %copy-start.2 = (f32[512]{0:T(512)S(1)}, f32[512]{0:T(512)}, u32[]{:S(2)}) copy-start(f32[512]{0:T(512)} %param.8) | copy-start | bytes 6148
  3.0 0.7 %copy-start.3 = (f32[512]{0:T(512)S(1)}, f32[512]{0:T(512)}, u32[]{:S(2)}) copy-start(f32[512]{0:T(512)} %param.9) | copy-start | bytes 6148
where the time goes:
time: 35.5 us; the launch traced here: 35.3 us
  Pallas kernels  30.7 us (86%)
  local copies, waits for them, and re-layouts  4.61 us (13%)
    pallas_call x1, Pallas kernels, local(): pl.pallas_call(kernel, out_shape=jax.ShapeDtypeStruct((ROWS, COLS), BF16)...  30.7 us
    unnamed x9, local copies, waits for them, and re-layouts  4.61 us

commit v1 on v0

--- a/solution.py
+++ b/solution.py
@@ -25,7 +25,9 @@
 COLS = 1024
 LANES = 128
 GT = GP // LANES
-OT = COLS // LANES
+HALVES = 2
+HALF = ROWS // HALVES
+CN = 256
 PLANE = 16
 DEPTH = 8
 PLANE_ORDER = sorted(range(1, PLANE), key=lambda d: -(min(d % 4, 4 - d % 4) + min(d // 4, 4 - d // 4)))
@@ -37,10 +39,10 @@
 
 
 def kernel(
-    x_hbm, w_hbm, dec_ref, frq_ref, r_hbm, skip_ref, out_hbm,
-    x_v, w_raw, w_v, r_own, r_sib, drive, ends, excl, packed, packed_sib, acc, out_v,
+    x_hbm, w_hbm, dec_hbm, frq_hbm, r_hbm, skip_hbm, out_hbm,
+    dec_ref, frq_ref, skip_ref, x_v, w_raw, w_v, r_own, r_sib, drive, enter, excl, packed, packed_sib, acc, out_v,
     plane_buf, depth_buf, lam_tab, pow_tab, dep_tab,
-    x_sem, w_sem, r_sem, o_sem, rs_send, rs_recv, pl_send, pl_recv, dp_send, dp_recv, pk_send, pk_recv,
+    s_sem, x_sem, w_sem, r_sem, o_sem, rs_send, rs_recv, pl_send, pl_recv, dp_send, dp_recv, pk_send, pk_recv, ready_sem,
 ):
     me, core = lax.axis_index("seq"), lax.axis_index("state")
     spot, deep = lax.rem(me, PLANE), lax.div(me, PLANE)
@@ -50,14 +52,37 @@
         spot_to = lax.rem(py + d // 4, 4) * 4 + lax.rem(px + d % 4, 4)
         return (deep * PLANE + spot_to, core), spot_to
 
-    def plane_from(d):
-        return lax.rem(py + 4 - d // 4, 4) * 4 + lax.rem(px + 4 - d % 4, 4)
-
     def depth_peer(d):
-        return (lax.rem(deep + d, DEPTH) * PLANE + spot, core)
+        return ((deep + d) * PLANE + spot, core)
 
     sibling = (me, 1 - core)
 
+    barrier = pltpu.get_barrier_semaphore()
+    for d in PLANE_ORDER:
+        pl.semaphore_signal(barrier, inc=1, device_id=plane_peer(d)[0], device_id_type=MESH_ID)
+    pl.semaphore_signal(barrier, inc=1, device_id=sibling, device_id_type=MESH_ID)
+
+    def after(d, act):
+        pl.when(deep + d < DEPTH)(act)
+
+    def before(d, act):
+        pl.when(deep - d >= 0)(act)
+
+    def greet(d):
+        pl.semaphore_signal(barrier, inc=1, device_id=depth_peer(d), device_id_type=MESH_ID)
+
+    def answer(d):
+        pl.semaphore_signal(ready_sem, inc=1, device_id=depth_peer(-d), device_id_type=MESH_ID)
+
+    for d in DEPTH_ORDER:
+        after(d, functools.partial(greet, d))
+
+    small = [
+        pltpu.make_async_copy(src, dst, s_sem.at[n])
+        for n, (src, dst) in enumerate(((dec_hbm, dec_ref), (frq_hbm, frq_ref), (skip_hbm, skip_ref)))
+    ]
+    for cp in small:
+        cp.start()
     x_cps, w_cps = [], [[] for _ in range(GROUPS)]
     for k in range(KN):
         cp = pltpu.make_async_copy(x_hbm.at[:, pl.ds(KC * k, KC)], x_v.at[:, pl.ds(KC * k, KC)], x_sem.at[k])
@@ -82,13 +107,9 @@
             cp.start()
             r_cps.append(cp)
 
-    barrier = pltpu.get_barrier_semaphore()
-    for d in DEPTH_ORDER:
-        pl.semaphore_signal(barrier, inc=1, device_id=depth_peer(d), device_id_type=MESH_ID)
-    for d in PLANE_ORDER:
-        pl.semaphore_signal(barrier, inc=1, device_id=plane_peer(d)[0], device_id_type=MESH_ID)
-    pl.semaphore_signal(barrier, inc=1, device_id=sibling, device_id_type=MESH_ID)
-
+    depth_buf[...] = jnp.zeros_like(depth_buf)
+    for cp in small:
+        cp.wait()
     dec, frq = dec_ref[...], frq_ref[...]
     mod = jnp.exp(-dec)
     sq = dec * dec
@@ -167,21 +188,25 @@
             nr = lr * sr - li * si + gg * jnp.concatenate(tiles[:GT], axis=1)
             ni = lr * si + li * sr + gg * jnp.concatenate(tiles[GT:], axis=1)
             sr, si = nr, ni
-            ends[g, pl.ds(CHUNKS * i, CHUNKS), pl.ds(0, GP)] = sr
-            ends[g, pl.ds(CHUNKS * i, CHUNKS), pl.ds(GP, GP)] = si
+            for t in range(GT):
+                drive[g, t, pl.ds(i, CHUNKS, stride=SUB), :] = sr[:, LANES * t : LANES * (t + 1)]
+                drive[g, GT + t, pl.ds(i, CHUNKS, stride=SUB), :] = si[:, LANES * t : LANES * (t + 1)]
         for d in (1, 2, 4):
             mr = jnp.where(step_of >= d, subs[d][0][:, GP * g : GP * (g + 1)], 0.0)
             mi = jnp.where(step_of >= d, subs[d][1][:, GP * g : GP * (g + 1)], 0.0)
             tr, ti = pltpu.roll(sr, d, 0), pltpu.roll(si, d, 0)
             sr, si = sr + mr * tr - mi * ti, si + mr * ti + mi * tr
-        for s in range(SEQS):
-            plane_buf[g, spot, pl.ds(s, 1), :] = sr[8 * s + 7 : 8 * s + 8]
-            plane_buf[g, spot, pl.ds(4 + s, 1), :] = si[8 * s + 7 : 8 * s + 8]
+        last = [v[8 * s + 7 : 8 * s + 8] for v in (sr, si) for s in range(SEQS)]
+        last = jnp.concatenate(last, axis=0)
+        tiles = [last[:, LANES * t : LANES * (t + 1)] for t in range(GT)]
+        plane_buf[g, spot] = jnp.concatenate(tiles, axis=0)
         excl[g, 0] = jnp.where(step_of >= 1, pltpu.roll(sr, 1, 0), 0.0)
         excl[g, 1] = jnp.where(step_of >= 1, pltpu.roll(si, 1, 0), 0.0)
 
         if g == 0:
-            pl.semaphore_wait(barrier, DEPTH + PLANE - 1)
+            pl.semaphore_wait(barrier, PLANE + deep)
+            for d in DEPTH_ORDER:
+                before(d, functools.partial(answer, d))
         for d in PLANE_ORDER:
             cp = pltpu.make_async_remote_copy(
                 src_ref=plane_buf.at[g, spot], dst_ref=plane_buf.at[g, spot], send_sem=pl_send.at[g, d],
@@ -189,7 +214,7 @@
             )
             cp.start()
             plane_cps[g].append(cp)
-        if g == GROUPS - 1:
+        if g == 0:
             for h in range(GROUPS):
                 for c in range(2):
                     cp = pltpu.make_async_remote_copy(
@@ -205,21 +230,28 @@
         lanes = pl.ds(GP * g, GP)
         for cp in plane_cps[g]:
             cp.wait_recv()
-        parts = [plane_buf[g, n] for n in range(PLANE)]
+        parts = [plane_buf[g, n].astype(F32) for n in range(PLANE)]
+        parts = [jnp.concatenate([p[8 * t : 8 * (t + 1)] for t in range(GT)], axis=1) for p in parts]
         depth_buf[g, deep] = weighted(parts, lam_tab, [PLANE - 1 - n for n in range(PLANE)], lanes)
+        if g == 0:
+
+            @pl.when(deep < DEPTH - 1)
+            def _():
+                pl.semaphore_wait(ready_sem, DEPTH - 1 - deep)
+
         for d in DEPTH_ORDER:
             cp = pltpu.make_async_remote_copy(
                 src_ref=depth_buf.at[g, deep], dst_ref=depth_buf.at[g, deep], send_sem=dp_send.at[g, d],
                 recv_sem=dp_recv.at[g, d], device_id=depth_peer(d), device_id_type=MESH_ID,
             )
-            cp.start()
-            depth_cps[g].append(cp)
+            after(d, cp.start)
+            depth_cps[g].append((d, cp))
         lam_re, lam_im = lam_tab[0, pl.ds(1, 1), lanes], lam_tab[1, pl.ds(1, 1), lanes] * sign
-        before = jnp.zeros((8, GP), F32)
+        pre = jnp.zeros((8, GP), F32)
         for n in range(PLANE - 1):
-            longer = lam_re * before + lam_im * pltpu.roll(before, 4, 0) + parts[n]
-            before = jnp.where(n < spot, longer, before)
-        entering.append(before)
+            longer = lam_re * pre + lam_im * pltpu.roll(pre, 4, 0) + parts[n]
+            pre = jnp.where(n < spot, longer, pre)
+        entering.append(pre)
     for cp in r_cps:
         cp.wait()
     for cp in rs_cps:
@@ -228,8 +260,8 @@
     skip = skip_ref[...]
     for g in range(GROUPS):
         lanes = pl.ds(GP * g, GP)
-        for cp in depth_cps[g]:
-            cp.wait_recv()
+        for d, cp in depth_cps[g]:
+            before(d, cp.wait_recv)
         come = entering[g] + weighted([depth_buf[g, n] for n in range(DEPTH)], dep_tab, list(range(DEPTH)), lanes)
         cr = jnp.concatenate([jnp.broadcast_to(come[s : s + 1], (8, GP)) for s in range(SEQS)], axis=0)
         ci = jnp.concatenate([jnp.broadcast_to(come[4 + s : 5 + s], (8, GP)) for s in range(SEQS)], axis=0)
@@ -237,79 +269,86 @@
         qi = jnp.concatenate([sub_im[:, GP * g : GP * (g + 1)]] * SEQS, axis=0)
         tr = excl[g, 0] + qr * cr - qi * ci
         ti = excl[g, 1] + qr * ci + qi * cr
-        for i in range(SUB):
-            ar, ai = pow_tab[0, pl.ds(i, 1), lanes], pow_tab[1, pl.ds(i, 1), lanes]
-            rows = pl.ds(CHUNKS * i, CHUNKS)
-            packed[g, rows, pl.ds(0, GP)] = (ends[g, rows, pl.ds(0, GP)] + ar * tr - ai * ti).astype(BF16)
-            packed[g, rows, pl.ds(GP, GP)] = (ends[g, rows, pl.ds(GP, GP)] + ar * ti + ai * tr).astype(BF16)
-        cp = pltpu.make_async_remote_copy(
-            src_ref=packed.at[g], dst_ref=packed_sib.at[g], send_sem=pk_send.at[g], recv_sem=pk_recv.at[g],
-            device_id=sibling, device_id_type=MESH_ID,
-        )
-        cp.start()
-        pack_cps.append(cp)
+        enter[g, 0], enter[g, 1] = tr, ti
+        ar, ai = pow_tab[0, :, lanes], pow_tab[1, :, lanes]
+        for h in range(HALVES):
+            for q in range(CHUNKS // HALVES * h, CHUNKS // HALVES * (h + 1)):
+                rows = pl.ds(SUB * q, SUB)
+                br, bi = enter[g, 0, pl.ds(q, 1), :], enter[g, 1, pl.ds(q, 1), :]
+                er = jnp.concatenate([drive[g, t, rows, :] for t in range(GT)], axis=1)
+                ei = jnp.concatenate([drive[g, GT + t, rows, :] for t in range(GT)], axis=1)
+                packed[g, rows, pl.ds(0, GP)] = (er + ar * br - ai * bi).astype(BF16)
+                packed[g, rows, pl.ds(GP, GP)] = (ei + ar * bi + ai * br).astype(BF16)
+            rows = pl.ds(HALF * h, HALF)
+            cp = pltpu.make_async_remote_copy(
+                src_ref=packed.at[g, rows], dst_ref=packed_sib.at[g, rows], send_sem=pk_send.at[g, h],
+                recv_sem=pk_recv.at[g, h], device_id=sibling, device_id_type=MESH_ID,
+            )
+            cp.start()
+            pack_cps.append(cp)
         part = jnp.dot(packed[g], r_own[g], preferred_element_type=F32)
-        for t in range(OT):
-            tile = part[:, LANES * t : LANES * (t + 1)]
-            acc[t] = tile if g == 0 else acc[t] + tile
-        cp.wait_recv()
+        if g == 0:
+            straight = x_v[:, pl.ds(my_cols, COLS)].astype(F32) * skip
+            acc[...] = part + straight
+        else:
+            acc[...] += part
         if g < GROUPS - 1:
-            part = jnp.dot(packed_sib[g], r_sib[g], preferred_element_type=F32)
-            for t in range(OT):
-                acc[t] += part[:, LANES * t : LANES * (t + 1)]
+            for cp in pack_cps[-HALVES:]:
+                cp.wait_recv()
+            acc[...] += jnp.dot(packed_sib[g], r_sib[g], preferred_element_type=F32)
     out_cps = []
     last = GROUPS - 1
-    CN = 256
-    for c in range(COLS // CN):
-        part = jnp.dot(packed_sib[last], r_sib[last, :, pl.ds(CN * c, CN)], preferred_element_type=F32)
-        of_chunk = range(CN // LANES * c, CN // LANES * (c + 1))
-        for n, t in enumerate(of_chunk):
-            acc[t] += part[:, LANES * n : LANES * (n + 1)]
-        gain = skip[:, CN * c : CN * (c + 1)]
-        from_col = pl.multiple_of(core * COLS + CN * c, CN)
-        for q in range(CHUNKS):
-            straight = x_v[pl.ds(SUB * q, SUB), pl.ds(from_col, CN)].astype(F32) * gain
-            summed = jnp.concatenate([acc[t, pl.ds(q, SUB, stride=CHUNKS), :] for t in of_chunk], axis=1)
-            out_v[pl.ds(SUB * q, SUB), pl.ds(CN * c, CN)] = (summed + straight).astype(BF16)
-        cp = pltpu.make_async_copy(out_v.at[:, pl.ds(CN * c, CN)], out_hbm.at[:, pl.ds(CN * c, CN)], o_sem.at[c])
+    for h in range(HALVES):
+        pack_cps[h - HALVES].wait_recv()
+        rows = pl.ds(HALF * h, HALF)
+        for c in range(COLS // CN):
+            cols = pl.ds(CN * c, CN)
+            part = jnp.dot(packed_sib[last, rows, :], r_sib[last, :, cols], preferred_element_type=F32)
+            out_v[rows, cols] = (acc[rows, cols] + part).astype(BF16)
+        cp = pltpu.make_async_copy(out_v.at[rows], out_hbm.at[rows], o_sem.at[h])
         cp.start()
         out_cps.append(cp)
     for cp in out_cps:
         cp.wait()
     for g in range(GROUPS):
-        for cp in plane_cps[g] + depth_cps[g]:
+        for cp in plane_cps[g]:
             cp.wait_send()
+        for d, cp in depth_cps[g]:
+            after(d, cp.wait_send)
     for cp in pack_cps + rs_cps:
         cp.wait_send()
 
 
 def local(inputs, in_proj, decay_rate, frequency, readout, skip_gain):
-    vmem = pl.BlockSpec(memory_space=pltpu.VMEM)
-    hbm = pl.BlockSpec(memory_space=pl.ANY)
+    hbm = pl.BlockSpec(memory_space=pltpu.HBM)
     dma = pltpu.SemaphoreType.DMA
     out = pl.pallas_call(
         kernel,
         out_shape=jax.ShapeDtypeStruct((ROWS, COLS), BF16),
-        in_specs=[hbm, hbm, vmem, vmem, hbm, vmem],
-        out_specs=hbm,
+        in_specs=[hbm] * 6,
+        out_specs=pl.BlockSpec(memory_space=pl.ANY),
         scratch_shapes=[
+            pltpu.VMEM((1, POLES), F32),
+            pltpu.VMEM((1, POLES), F32),
+            pltpu.VMEM((1, COLS), F32),
             pltpu.VMEM((ROWS, WIDTH), BF16),
             pltpu.VMEM((GROUPS, KN, KC, 2, GP), BF16),
             pltpu.VMEM((WIDTH, 2 * GP), BF16),
             pltpu.VMEM((GROUPS, 2 * GP, COLS), BF16),
             pltpu.VMEM((GROUPS, 2 * GP, COLS), BF16),
             pltpu.VMEM((GROUPS, 2 * GT, ROWS, LANES), F32),
-            pltpu.VMEM((GROUPS, ROWS, 2 * GP), F32),
+            pltpu.VMEM((GROUPS, 2, CHUNKS, GP), F32),
             pltpu.VMEM((GROUPS, 2, CHUNKS, GP), F32),
             pltpu.VMEM((GROUPS, ROWS, 2 * GP), BF16),
             pltpu.VMEM((GROUPS, ROWS, 2 * GP), BF16),
-            pltpu.VMEM((OT, ROWS, LANES), F32),
+            pltpu.VMEM((ROWS, COLS), F32),
             pltpu.VMEM((ROWS, COLS), BF16),
-            pltpu.VMEM((GROUPS, PLANE, 8, GP), F32),
+            pltpu.VMEM((GROUPS, PLANE, 8 * GT, LANES), F32),
             pltpu.VMEM((GROUPS, DEPTH, 8, GP), F32),
             pltpu.VMEM((2, PLANE, POLES), F32),
             pltpu.VMEM((2, SUB, POLES), F32),
             pltpu.VMEM((2, DEPTH, POLES), F32),
+            dma((3,)),
             dma((KN,)),
             dma((GROUPS, KN)),
             dma((GROUPS, 2)),
@@ -320,11 +359,12 @@
             dma((GROUPS, PLANE)),
             dma((GROUPS, DEPTH)),
             dma((GROUPS, DEPTH)),
-            dma((GROUPS,)),
-            dma((GROUPS,)),
+            dma((GROUPS, HALVES)),
+            dma((GROUPS, HALVES)),
+            pltpu.SemaphoreType.REGULAR,
         ],
         compiler_params=pltpu.CompilerParams(
-            collective_id=0, has_side_effects=True, vmem_limit_bytes=48 << 20
+            collective_id=0, has_side_effects=True, vmem_limit_bytes=64 << 20
         ),
     )(
         inputs.reshape(ROWS, WIDTH), in_proj, decay_rate.reshape(1, POLES), frequency.reshape(1, POLES),

time: 35.5 us -> 27.5 us (0.77)
  the two profiles are of different devices: /device:TPU:1 before, /device:TPU:225 now
where the time goes in v1:
time: 27.5 us; the launch traced here: 27.4 us
  Pallas kernels  25.1 us (91%)
  local copies, waits for them, and re-layouts  2.26 us (8%)
    pallas_call x1, Pallas kernels, local(): pl.pallas_call(kernel, out_shape=jax.ShapeDtypeStruct((ROWS, COLS), BF16)...  25.1 us
    unnamed x1, local copies, waits for them, and re-layouts  2.26 us

profile of v1, /device:TPU:225, one launch (start us, length us, event | category | flops | bytes accessed | tf_op | source)
XLA Modules:
  0.0 27.4 jit_solution(11824933750056560)
XLA Ops:
  0.0 25.1 %shard_map.64 = bf16[512,1024]{1,0:T(8,128)(2,1)} custom-call(bf16[512,2048]{1,0:T(8,128)(2,1)} %bitcast.6, bf16[2048,2,512]{2,1,0:T(2,128)(2,1)} %w_hbm.1, f32[1,512]{1,0:T(1,128)} %bitcast.8, f32[1,512]{1,0:T(1,128)} %bitcast.9, bf16[2,512,2048]{2,1,0:T(8,128)(2,1)} %r_hbm.1, f32[1,1024]{1,0:T(1,128)} %bitcast.7), custom_call_target="tpu_custom_call" | custom-call | tf_op jit(solution)/shard_map/pallas_call | solution.py:325
  25.1 2.3 %copy.8 = bf16[4,128,1024]{2,1,0:T(8,128)(2,1)} copy(bf16[4,128,1024]{2,1,0:T(8,128)(2,1)} %bitcast.5) | data formatting | bytes 2097152

commit v2 on v1

--- a/solution.py
+++ b/solution.py
@@ -16,12 +16,14 @@
 ROWS = SEQS * STEPS
 WIDTH = 2048
 POLES = 512
-GROUPS = 2
+GROUPS = 1
 GP = POLES // GROUPS
 SUB = 16
 CHUNKS = ROWS // SUB
 KC = 512
 KN = WIDTH // KC
+AHEAD = 2
+PITCH = 17
 COLS = 1024
 LANES = 128
 GT = GP // LANES
@@ -39,10 +41,10 @@
 
 
 def kernel(
-    x_hbm, w_hbm, dec_hbm, frq_hbm, r_hbm, skip_hbm, out_hbm,
-    dec_ref, frq_ref, skip_ref, x_v, w_raw, w_v, r_own, r_sib, drive, enter, excl, packed, packed_sib, acc, out_v,
+    x_hbm, w_hbm, dec_hbm, frq_hbm, r_hbm, skip_hbm, out_v,
+    dec_ref, frq_ref, skip_ref, x_v, w_raw, w_v, r_own, r_sib, drive, enter, excl, packed, packed_sib, acc,
     plane_buf, depth_buf, lam_tab, pow_tab, dep_tab,
-    s_sem, x_sem, w_sem, r_sem, o_sem, rs_send, rs_recv, pl_send, pl_recv, dp_send, dp_recv, pk_send, pk_recv, ready_sem,
+    s_sem, x_sem, w_sem, r_sem, rs_send, rs_recv, pl_send, pl_recv, dp_send, dp_recv, pk_send, pk_recv, ready_sem,
 ):
     me, core = lax.axis_index("seq"), lax.axis_index("state")
     spot, deep = lax.rem(me, PLANE), lax.div(me, PLANE)
@@ -56,26 +58,6 @@
         return ((deep + d) * PLANE + spot, core)
 
     sibling = (me, 1 - core)
-
-    barrier = pltpu.get_barrier_semaphore()
-    for d in PLANE_ORDER:
-        pl.semaphore_signal(barrier, inc=1, device_id=plane_peer(d)[0], device_id_type=MESH_ID)
-    pl.semaphore_signal(barrier, inc=1, device_id=sibling, device_id_type=MESH_ID)
-
-    def after(d, act):
-        pl.when(deep + d < DEPTH)(act)
-
-    def before(d, act):
-        pl.when(deep - d >= 0)(act)
-
-    def greet(d):
-        pl.semaphore_signal(barrier, inc=1, device_id=depth_peer(d), device_id_type=MESH_ID)
-
-    def answer(d):
-        pl.semaphore_signal(ready_sem, inc=1, device_id=depth_peer(-d), device_id_type=MESH_ID)
-
-    for d in DEPTH_ORDER:
-        after(d, functools.partial(greet, d))
 
     small = [
         pltpu.make_async_copy(src, dst, s_sem.at[n])
@@ -83,29 +65,59 @@
     ]
     for cp in small:
         cp.start()
-    x_cps, w_cps = [], [[] for _ in range(GROUPS)]
-    for k in range(KN):
-        cp = pltpu.make_async_copy(x_hbm.at[:, pl.ds(KC * k, KC)], x_v.at[:, pl.ds(KC * k, KC)], x_sem.at[k])
-        cp.start()
-        x_cps.append(cp)
-        cp = pltpu.make_async_copy(w_hbm.at[pl.ds(KC * k, KC), :, pl.ds(0, GP)], w_raw.at[0, k], w_sem.at[0, k])
-        cp.start()
-        w_cps[0].append(cp)
-    for g in range(1, GROUPS):
-        for k in range(KN):
-            cp = pltpu.make_async_copy(w_hbm.at[pl.ds(KC * k, KC), :, pl.ds(GP * g, GP)], w_raw.at[g, k], w_sem.at[g, k])
-            cp.start()
-            w_cps[g].append(cp)
+    x_cps = [
+        pltpu.make_async_copy(x_hbm.at[:, pl.ds(KC * k, KC)], x_v.at[:, pl.ds(KC * k, KC)], x_sem.at[k])
+        for k in range(KN)
+    ]
+    w_cps = [
+        [
+            pltpu.make_async_copy(w_hbm.at[pl.ds(KC * k, KC), :, pl.ds(GP * g, GP)], w_raw.at[g, k], w_sem.at[g, k])
+            for k in range(KN)
+        ]
+        for g in range(GROUPS)
+    ]
+
+    def bring(n):
+        if n < KN * GROUPS:
+            g, k = divmod(n, KN)
+            w_cps[g][k].start()
+            if g == 0:
+                x_cps[k].start()
+        elif n == KN * GROUPS:
+            for cp in r_cps:
+                cp.start()
+
+    for n in range(AHEAD):
+        bring(n)
     my_cols = pl.multiple_of(core * COLS, COLS)
     sib_cols = pl.multiple_of((1 - core) * COLS, COLS)
-    r_cps = []
-    for g in range(GROUPS):
-        for c in range(2):
-            cp = pltpu.make_async_copy(
-                r_hbm.at[c, pl.ds(GP * g, GP), pl.ds(my_cols, COLS)], r_own.at[g, pl.ds(GP * c, GP)], r_sem.at[g, c]
-            )
-            cp.start()
-            r_cps.append(cp)
+    r_cps = [
+        pltpu.make_async_copy(
+            r_hbm.at[c, pl.ds(GP * g, GP), pl.ds(my_cols, COLS)], r_own.at[g, pl.ds(GP * c, GP)], r_sem.at[g, c]
+        )
+        for g in range(GROUPS)
+        for c in range(2)
+    ]
+
+    barrier = pltpu.get_barrier_semaphore()
+    for d in PLANE_ORDER:
+        pl.semaphore_signal(barrier, inc=1, device_id=plane_peer(d)[0], device_id_type=MESH_ID)
+    pl.semaphore_signal(barrier, inc=1, device_id=sibling, device_id_type=MESH_ID)
+
+    def after(d, act):
+        pl.when(deep + d < DEPTH)(act)
+
+    def before(d, act):
+        pl.when(deep - d >= 0)(act)
+
+    def greet(d):
+        pl.semaphore_signal(barrier, inc=1, device_id=depth_peer(d), device_id_type=MESH_ID)
+
+    def answer(d):
+        pl.semaphore_signal(ready_sem, inc=1, device_id=depth_peer(-d), device_id_type=MESH_ID)
+
+    for d in DEPTH_ORDER:
+        after(d, functools.partial(greet, d))
 
     depth_buf[...] = jnp.zeros_like(depth_buf)
     for cp in small:
@@ -159,38 +171,47 @@
 
     plane_cps, depth_cps, pack_cps, rs_cps = [[] for _ in range(GROUPS)], [[] for _ in range(GROUPS)], [], []
 
-    for k in range(KN):
-        x_cps[k].wait()
-    for g in range(GROUPS):
+    def turn(g, k):
+        for at in range(0, KC, 16):
+            both = jnp.swapaxes(w_raw[g, k, pl.ds(at, 16)], 0, 1)
+            w_v[g, pl.ds(KC * k + at, 16), pl.ds(0, GP)] = both[0]
+            w_v[g, pl.ds(KC * k + at, 16), pl.ds(GP, GP)] = both[1]
+
+    def fetch(g, k):
+        w_cps[g][k].wait()
+        if g == 0:
+            x_cps[k].wait()
+        bring(KN * g + k + AHEAD)
+        turn(g, k)
+
+    todo = [(g, n) for g in range(GROUPS) for n in range(KN)]
+    fetch(*todo[0])
+    for at, (g, n) in enumerate(todo):
         lanes = pl.ds(GP * g, GP)
-        for k in range(KN):
-            w_cps[g][k].wait()
-
-            def turn(n, carry):
-                for u in range(4):
-                    at = pl.multiple_of(n * 64 + u * 16, 16)
-                    both = jnp.swapaxes(w_raw[g, k, pl.ds(at, 16)], 0, 1)
-                    w_v[pl.ds(KC * k + at, 16), pl.ds(0, GP)] = both[0]
-                    w_v[pl.ds(KC * k + at, 16), pl.ds(GP, GP)] = both[1]
-                return carry
-
-            lax.fori_loop(0, KC // 64, turn, 0)
-        driven = jnp.dot(x_v[...], w_v[...], preferred_element_type=F32)
+        if at + 1 < len(todo):
+            fetch(*todo[at + 1])
+        deep_part = pl.ds(KC * n, KC)
+        driven = jnp.dot(x_v[:, deep_part], w_v[g, deep_part, :], preferred_element_type=F32)
         for t in range(2 * GT):
-            drive[g, t] = driven[:, LANES * t : LANES * (t + 1)]
+            tile = driven[:, LANES * t : LANES * (t + 1)]
+            for q in range(CHUNKS):
+                rows, piece = pl.ds(PITCH * q, SUB), tile[SUB * q : SUB * (q + 1)]
+                drive[g, t, rows, :] = piece if n == 0 else drive[g, t, rows, :] + piece
+        if n + 1 < KN:
+            continue
 
         lr, li = base[0][:, GP * g : GP * (g + 1)], base[1][:, GP * g : GP * (g + 1)]
         gg = gam[:, GP * g : GP * (g + 1)]
         sr = jnp.zeros((CHUNKS, GP), F32)
         si = jnp.zeros((CHUNKS, GP), F32)
         for i in range(SUB):
-            tiles = [drive[g, t, pl.ds(i, CHUNKS, stride=SUB), :] for t in range(2 * GT)]
+            tiles = [drive[g, t, pl.ds(i, CHUNKS, stride=PITCH), :] for t in range(2 * GT)]
             nr = lr * sr - li * si + gg * jnp.concatenate(tiles[:GT], axis=1)
             ni = lr * si + li * sr + gg * jnp.concatenate(tiles[GT:], axis=1)
             sr, si = nr, ni
             for t in range(GT):
-                drive[g, t, pl.ds(i, CHUNKS, stride=SUB), :] = sr[:, LANES * t : LANES * (t + 1)]
-                drive[g, GT + t, pl.ds(i, CHUNKS, stride=SUB), :] = si[:, LANES * t : LANES * (t + 1)]
+                drive[g, t, pl.ds(i, CHUNKS, stride=PITCH), :] = sr[:, LANES * t : LANES * (t + 1)]
+                drive[g, GT + t, pl.ds(i, CHUNKS, stride=PITCH), :] = si[:, LANES * t : LANES * (t + 1)]
         for d in (1, 2, 4):
             mr = jnp.where(step_of >= d, subs[d][0][:, GP * g : GP * (g + 1)], 0.0)
             mi = jnp.where(step_of >= d, subs[d][1][:, GP * g : GP * (g + 1)], 0.0)
@@ -214,7 +235,7 @@
             )
             cp.start()
             plane_cps[g].append(cp)
-        if g == 0:
+        if g == GROUPS - 1:
             for h in range(GROUPS):
                 for c in range(2):
                     cp = pltpu.make_async_remote_copy(
@@ -275,8 +296,9 @@
             for q in range(CHUNKS // HALVES * h, CHUNKS // HALVES * (h + 1)):
                 rows = pl.ds(SUB * q, SUB)
                 br, bi = enter[g, 0, pl.ds(q, 1), :], enter[g, 1, pl.ds(q, 1), :]
-                er = jnp.concatenate([drive[g, t, rows, :] for t in range(GT)], axis=1)
-                ei = jnp.concatenate([drive[g, GT + t, rows, :] for t in range(GT)], axis=1)
+                held = pl.ds(PITCH * q, SUB)
+                er = jnp.concatenate([drive[g, t, held, :] for t in range(GT)], axis=1)
+                ei = jnp.concatenate([drive[g, GT + t, held, :] for t in range(GT)], axis=1)
                 packed[g, rows, pl.ds(0, GP)] = (er + ar * br - ai * bi).astype(BF16)
                 packed[g, rows, pl.ds(GP, GP)] = (ei + ar * bi + ai * br).astype(BF16)
             rows = pl.ds(HALF * h, HALF)
@@ -296,7 +318,6 @@
             for cp in pack_cps[-HALVES:]:
                 cp.wait_recv()
             acc[...] += jnp.dot(packed_sib[g], r_sib[g], preferred_element_type=F32)
-    out_cps = []
     last = GROUPS - 1
     for h in range(HALVES):
         pack_cps[h - HALVES].wait_recv()
@@ -305,11 +326,6 @@
             cols = pl.ds(CN * c, CN)
             part = jnp.dot(packed_sib[last, rows, :], r_sib[last, :, cols], preferred_element_type=F32)
             out_v[rows, cols] = (acc[rows, cols] + part).astype(BF16)
-        cp = pltpu.make_async_copy(out_v.at[rows], out_hbm.at[rows], o_sem.at[h])
-        cp.start()
-        out_cps.append(cp)
-    for cp in out_cps:
-        cp.wait()
     for g in range(GROUPS):
         for cp in plane_cps[g]:
             cp.wait_send()
@@ -324,25 +340,24 @@
     dma = pltpu.SemaphoreType.DMA
     out = pl.pallas_call(
         kernel,
-        out_shape=jax.ShapeDtypeStruct((ROWS, COLS), BF16),
+        out_shape=pltpu.VMEM((ROWS, COLS), BF16),
         in_specs=[hbm] * 6,
-        out_specs=pl.BlockSpec(memory_space=pl.ANY),
+        out_specs=pl.BlockSpec(memory_space=pltpu.VMEM),
         scratch_shapes=[
             pltpu.VMEM((1, POLES), F32),
             pltpu.VMEM((1, POLES), F32),
             pltpu.VMEM((1, COLS), F32),
             pltpu.VMEM((ROWS, WIDTH), BF16),
             pltpu.VMEM((GROUPS, KN, KC, 2, GP), BF16),
-            pltpu.VMEM((WIDTH, 2 * GP), BF16),
+            pltpu.VMEM((GROUPS, WIDTH, 2 * GP), BF16),
             pltpu.VMEM((GROUPS, 2 * GP, COLS), BF16),
             pltpu.VMEM((GROUPS, 2 * GP, COLS), BF16),
-            pltpu.VMEM((GROUPS, 2 * GT, ROWS, LANES), F32),
+            pltpu.VMEM((GROUPS, 2 * GT, CHUNKS * PITCH + SUB, LANES), F32),
             pltpu.VMEM((GROUPS, 2, CHUNKS, GP), F32),
             pltpu.VMEM((GROUPS, 2, CHUNKS, GP), F32),
             pltpu.VMEM((GROUPS, ROWS, 2 * GP), BF16),
             pltpu.VMEM((GROUPS, ROWS, 2 * GP), BF16),
             pltpu.VMEM((ROWS, COLS), F32),
-            pltpu.VMEM((ROWS, COLS), BF16),
             pltpu.VMEM((GROUPS, PLANE, 8 * GT, LANES), F32),
             pltpu.VMEM((GROUPS, DEPTH, 8, GP), F32),
             pltpu.VMEM((2, PLANE, POLES), F32),
@@ -352,7 +367,6 @@
             dma((KN,)),
             dma((GROUPS, KN)),
             dma((GROUPS, 2)),
-            dma((4,)),
             dma((GROUPS, 2)),
             dma((GROUPS, 2)),
             dma((GROUPS, PLANE)),
@@ -364,11 +378,16 @@
             pltpu.SemaphoreType.REGULAR,
         ],
         compiler_params=pltpu.CompilerParams(
-            collective_id=0, has_side_effects=True, vmem_limit_bytes=64 << 20
+            collective_id=0, has_side_effects=True, vmem_limit_bytes=40 << 20
         ),
     )(
-        inputs.reshape(ROWS, WIDTH), in_proj, decay_rate.reshape(1, POLES), frequency.reshape(1, POLES),
-        readout, skip_gain.reshape(1, COLS),
+        *[
+            pltpu.with_memory_space_constraint(part, pltpu.HBM)
+            for part in (
+                inputs.reshape(ROWS, WIDTH), in_proj, decay_rate.reshape(1, POLES), frequency.reshape(1, POLES),
+                readout, skip_gain.reshape(1, COLS),
+            )
+        ]
     )
     return out.reshape(SEQS, STEPS, COLS)
 

time: 27.5 us -> 22.7 us (0.83)
  Pallas kernels: 25.1 us -> 21.6 us
  local copies, waits for them, and re-layouts: 2.26 us -> 0.97 us
    pallas_call x1, Pallas kernels: 25.1 us -> 21.6 us  [local(): pl.pallas_call(kernel, out_shape=pltpu.VMEM((ROWS, COLS), BF16), in_specs...]
    unnamed x1, local copies, waits for them, and re-layouts: 2.26 us -> 0.97 us
where the time goes in v2:
time: 22.7 us; the launch traced here: 22.6 us
  Pallas kernels  21.6 us (95%)
  local copies, waits for them, and re-layouts  0.97 us (4%)
    pallas_call x1, Pallas kernels, local(): pl.pallas_call(kernel, out_shape=pltpu.VMEM((ROWS, COLS), BF16), in_specs...  21.6 us
    unnamed x1, local copies, waits for them, and re-layouts  0.97 us

profile of v2, /device:TPU:225, one launch (start us, length us, event | category | flops | bytes accessed | tf_op | source)
XLA Modules:
  0.0 22.6 jit_solution(6640790626654584674)
XLA Ops:
  0.0 21.6 %shard_map.64 = bf16[512,1024]{1,0:T(8,128)(2,1)S(1)} custom-call(bf16[512,2048]{1,0:T(8,128)(2,1)} %bitcast.6, bf16[2048,2,512]{2,1,0:T(2,128)(2,1)} %w_hbm.1, f32[1,512]{1,0:T(1,128)} %bitcast.8, f32[1,512]{1,0:T(1,128)} %bitcast.9, bf16[2,512,2048]{2,1,0:T(8,128)(2,1)} %r_hbm.1, f32[1,1024]{1,0:T(1,128)} %bitcast.7), custom_call_target="tpu_custom_call" | custom-call | tf_op jit(solution)/shard_map/pallas_call | solution.py:341
  21.6 1.0 %copy.8 = bf16[4,128,1024]{2,1,0:T(8,128)(2,1)} copy(bf16[4,128,1024]{2,1,0:T(8,128)(2,1)S(1)} %bitcast.5) | data formatting | bytes 2097152

commit v3 on v2

--- a/solution.py
+++ b/solution.py
@@ -20,14 +20,15 @@
 GP = POLES // GROUPS
 SUB = 16
 CHUNKS = ROWS // SUB
-KC = 512
+KC = 256
 KN = WIDTH // KC
-AHEAD = 2
+AHEAD = 4
 PITCH = 17
 COLS = 1024
 LANES = 128
 GT = GP // LANES
-HALVES = 2
+HALVES = 4
+PIECES = 4
 HALF = ROWS // HALVES
 CN = 256
 PLANE = 16
@@ -43,7 +44,7 @@
 def kernel(
     x_hbm, w_hbm, dec_hbm, frq_hbm, r_hbm, skip_hbm, out_v,
     dec_ref, frq_ref, skip_ref, x_v, w_raw, w_v, r_own, r_sib, drive, enter, excl, packed, packed_sib, acc,
-    plane_buf, depth_buf, lam_tab, pow_tab, dep_tab,
+    plane_buf, depth_buf, lam_tab, pow_tab, dep_tab, pre_tab,
     s_sem, x_sem, w_sem, r_sem, rs_send, rs_recv, pl_send, pl_recv, dp_send, dp_recv, pk_send, pk_recv, ready_sem,
 ):
     me, core = lax.axis_index("seq"), lax.axis_index("state")
@@ -158,6 +159,14 @@
         dep_tab[0, pl.ds(n, 1), :] = weight[0]
         dep_tab[1, pl.ds(n, 1), :] = weight[1]
 
+    weight = (jnp.zeros_like(dec), jnp.zeros_like(dec))
+    for n in range(PLANE - 1, -1, -1):
+        longer = cmul(*weight, *lams[1])
+        first = spot - 1 == n
+        weight = tuple(jnp.where(first, h, w) for h, w in zip(one, longer))
+        pre_tab[0, pl.ds(n, 1), :] = weight[0]
+        pre_tab[1, pl.ds(n, 1), :] = weight[1]
+
     step_of = lax.rem(lax.broadcasted_iota(jnp.int32, (CHUNKS, GP), 0), 8)
     sign = jnp.where(lax.broadcasted_iota(jnp.int32, (8, GP), 0) < 4, -1.0, 1.0)
 
@@ -190,6 +199,10 @@
         lanes = pl.ds(GP * g, GP)
         if at + 1 < len(todo):
             fetch(*todo[at + 1])
+        if g == 0 and n == KN - 2:
+            pl.semaphore_wait(barrier, PLANE + deep)
+            for d in DEPTH_ORDER:
+                before(d, functools.partial(answer, d))
         deep_part = pl.ds(KC * n, KC)
         driven = jnp.dot(x_v[:, deep_part], w_v[g, deep_part, :], preferred_element_type=F32)
         for t in range(2 * GT):
@@ -224,10 +237,6 @@
         excl[g, 0] = jnp.where(step_of >= 1, pltpu.roll(sr, 1, 0), 0.0)
         excl[g, 1] = jnp.where(step_of >= 1, pltpu.roll(si, 1, 0), 0.0)
 
-        if g == 0:
-            pl.semaphore_wait(barrier, PLANE + deep)
-            for d in DEPTH_ORDER:
-                before(d, functools.partial(answer, d))
         for d in PLANE_ORDER:
             cp = pltpu.make_async_remote_copy(
                 src_ref=plane_buf.at[g, spot], dst_ref=plane_buf.at[g, spot], send_sem=pl_send.at[g, d],
@@ -235,16 +244,15 @@
             )
             cp.start()
             plane_cps[g].append(cp)
-        if g == GROUPS - 1:
-            for h in range(GROUPS):
-                for c in range(2):
-                    cp = pltpu.make_async_remote_copy(
-                        src_ref=r_hbm.at[c, pl.ds(GP * h, GP), pl.ds(sib_cols, COLS)],
-                        dst_ref=r_sib.at[h, pl.ds(GP * c, GP)], send_sem=rs_send.at[h, c],
-                        recv_sem=rs_recv.at[h, c], device_id=sibling, device_id_type=MESH_ID,
-                    )
-                    cp.start()
-                    rs_cps.append(cp)
+    for h in range(GROUPS):
+        for c in range(2):
+            cp = pltpu.make_async_remote_copy(
+                src_ref=r_hbm.at[c, pl.ds(GP * h, GP), pl.ds(sib_cols, COLS)],
+                dst_ref=r_sib.at[h, pl.ds(GP * c, GP)], send_sem=rs_send.at[h, c],
+                recv_sem=rs_recv.at[h, c], device_id=sibling, device_id_type=MESH_ID,
+            )
+            cp.start()
+            rs_cps.append(cp)
 
     entering = []
     for g in range(GROUPS):
@@ -267,18 +275,10 @@
             )
             after(d, cp.start)
             depth_cps[g].append((d, cp))
-        lam_re, lam_im = lam_tab[0, pl.ds(1, 1), lanes], lam_tab[1, pl.ds(1, 1), lanes] * sign
-        pre = jnp.zeros((8, GP), F32)
-        for n in range(PLANE - 1):
-            longer = lam_re * pre + lam_im * pltpu.roll(pre, 4, 0) + parts[n]
-            pre = jnp.where(n < spot, longer, pre)
-        entering.append(pre)
+        entering.append(weighted(parts, pre_tab, list(range(PLANE)), lanes))
     for cp in r_cps:
         cp.wait()
-    for cp in rs_cps:
-        cp.wait_recv()
-
-    skip = skip_ref[...]
+    acc[...] = x_v[:, pl.ds(my_cols, COLS)].astype(F32) * skip_ref[...]
     for g in range(GROUPS):
         lanes = pl.ds(GP * g, GP)
         for d, cp in depth_cps[g]:
@@ -292,8 +292,8 @@
         ti = excl[g, 1] + qr * ci + qi * cr
         enter[g, 0], enter[g, 1] = tr, ti
         ar, ai = pow_tab[0, :, lanes], pow_tab[1, :, lanes]
-        for h in range(HALVES):
-            for q in range(CHUNKS // HALVES * h, CHUNKS // HALVES * (h + 1)):
+        for h in range(PIECES):
+            for q in range(CHUNKS // PIECES * h, CHUNKS // PIECES * (h + 1)):
                 rows = pl.ds(SUB * q, SUB)
                 br, bi = enter[g, 0, pl.ds(q, 1), :], enter[g, 1, pl.ds(q, 1), :]
                 held = pl.ds(PITCH * q, SUB)
@@ -301,7 +301,7 @@
                 ei = jnp.concatenate([drive[g, GT + t, held, :] for t in range(GT)], axis=1)
                 packed[g, rows, pl.ds(0, GP)] = (er + ar * br - ai * bi).astype(BF16)
                 packed[g, rows, pl.ds(GP, GP)] = (ei + ar * bi + ai * br).astype(BF16)
-            rows = pl.ds(HALF * h, HALF)
+            rows = pl.ds(ROWS // PIECES * h, ROWS // PIECES)
             cp = pltpu.make_async_remote_copy(
                 src_ref=packed.at[g, rows], dst_ref=packed_sib.at[g, rows], send_sem=pk_send.at[g, h],
                 recv_sem=pk_recv.at[g, h], device_id=sibling, device_id_type=MESH_ID,
@@ -309,18 +309,18 @@
             cp.start()
             pack_cps.append(cp)
         part = jnp.dot(packed[g], r_own[g], preferred_element_type=F32)
+        acc[...] += part
         if g == 0:
-            straight = x_v[:, pl.ds(my_cols, COLS)].astype(F32) * skip
-            acc[...] = part + straight
-        else:
-            acc[...] += part
+            for cp in rs_cps:
+                cp.wait_recv()
         if g < GROUPS - 1:
-            for cp in pack_cps[-HALVES:]:
+            for cp in pack_cps[-PIECES:]:
                 cp.wait_recv()
             acc[...] += jnp.dot(packed_sib[g], r_sib[g], preferred_element_type=F32)
     last = GROUPS - 1
     for h in range(HALVES):
-        pack_cps[h - HALVES].wait_recv()
+        for n in range(PIECES // HALVES):
+            pack_cps[PIECES // HALVES * h + n - PIECES].wait_recv()
         rows = pl.ds(HALF * h, HALF)
         for c in range(COLS // CN):
             cols = pl.ds(CN * c, CN)
@@ -363,6 +363,7 @@
             pltpu.VMEM((2, PLANE, POLES), F32),
             pltpu.VMEM((2, SUB, POLES), F32),
             pltpu.VMEM((2, DEPTH, POLES), F32),
+            pltpu.VMEM((2, PLANE, POLES), F32),
             dma((3,)),
             dma((KN,)),
             dma((GROUPS, KN)),
@@ -373,8 +374,8 @@
             dma((GROUPS, PLANE)),
             dma((GROUPS, DEPTH)),
             dma((GROUPS, DEPTH)),
-            dma((GROUPS, HALVES)),
-            dma((GROUPS, HALVES)),
+            dma((GROUPS, PIECES)),
+            dma((GROUPS, PIECES)),
             pltpu.SemaphoreType.REGULAR,
         ],
         compiler_params=pltpu.CompilerParams(

time: 22.7 us -> 22.9 us (level)
  no operation moved by 1% of the time
where the time goes in v3:
time: 22.9 us; the launch traced here: 22.8 us
  Pallas kernels  21.8 us (95%)
  local copies, waits for them, and re-layouts  0.97 us (4%)
    pallas_call x1, Pallas kernels, local(): pl.pallas_call(kernel, out_shape=pltpu.VMEM((ROWS, COLS), BF16), in_specs...  21.8 us
    unnamed x1, local copies, waits for them, and re-layouts  0.97 us

profile of v3, /device:TPU:225, one launch (start us, length us, event | category | flops | bytes accessed | tf_op | source)
XLA Modules:
  0.0 22.8 jit_solution(18344216837002319393)
XLA Ops:
  0.0 21.8 %shard_map.64 = bf16[512,1024]{1,0:T(8,128)(2,1)S(1)} custom-call(bf16[512,2048]{1,0:T(8,128)(2,1)} %bitcast.6, bf16[2048,2,512]{2,1,0:T(2,128)(2,1)} %w_hbm.1, f32[1,512]{1,0:T(1,128)} %bitcast.8, f32[1,512]{1,0:T(1,128)} %bitcast.9, bf16[2,512,2048]{2,1,0:T(8,128)(2,1)} %r_hbm.1, f32[1,1024]{1,0:T(1,128)} %bitcast.7), custom_call_target="tpu_custom_call" | custom-call | tf_op jit(solution)/shard_map/pallas_call | solution.py:341
  21.8 1.0 %copy.8 = bf16[4,128,1024]{2,1,0:T(8,128)(2,1)} copy(bf16[4,128,1024]{2,1,0:T(8,128)(2,1)S(1)} %bitcast.5) | data formatting | bytes 2097152

commit v4 on v3

--- a/solution.py
+++ b/solution.py
@@ -27,8 +27,8 @@
 COLS = 1024
 LANES = 128
 GT = GP // LANES
-HALVES = 4
-PIECES = 4
+HALVES = 2
+PIECES = 2
 HALF = ROWS // HALVES
 CN = 256
 PLANE = 16
@@ -199,10 +199,6 @@
         lanes = pl.ds(GP * g, GP)
         if at + 1 < len(todo):
             fetch(*todo[at + 1])
-        if g == 0 and n == KN - 2:
-            pl.semaphore_wait(barrier, PLANE + deep)
-            for d in DEPTH_ORDER:
-                before(d, functools.partial(answer, d))
         deep_part = pl.ds(KC * n, KC)
         driven = jnp.dot(x_v[:, deep_part], w_v[g, deep_part, :], preferred_element_type=F32)
         for t in range(2 * GT):
@@ -237,6 +233,10 @@
         excl[g, 0] = jnp.where(step_of >= 1, pltpu.roll(sr, 1, 0), 0.0)
         excl[g, 1] = jnp.where(step_of >= 1, pltpu.roll(si, 1, 0), 0.0)
 
+        if g == 0:
+            pl.semaphore_wait(barrier, PLANE + deep)
+            for d in DEPTH_ORDER:
+                before(d, functools.partial(answer, d))
         for d in PLANE_ORDER:
             cp = pltpu.make_async_remote_copy(
                 src_ref=plane_buf.at[g, spot], dst_ref=plane_buf.at[g, spot], send_sem=pl_send.at[g, d],

time: 22.9 us -> 22.6 us (0.987)
    pallas_call x1, Pallas kernels: 21.8 us -> 21.6 us  [local(): pl.pallas_call(kernel, out_shape=pltpu.VMEM((ROWS, COLS), BF16), in_specs...]
where the time goes in v4:
time: 22.6 us; the launch traced here: 22.5 us
  Pallas kernels  21.6 us (96%)
  local copies, waits for them, and re-layouts  0.97 us (4%)
    pallas_call x1, Pallas kernels, local(): pl.pallas_call(kernel, out_shape=pltpu.VMEM((ROWS, COLS), BF16), in_specs...  21.6 us
    unnamed x1, local copies, waits for them, and re-layouts  0.97 us

profile of v4, /device:TPU:225, one launch (start us, length us, event | category | flops | bytes accessed | tf_op | source)
XLA Modules:
  0.0 22.5 jit_solution(2531701055893522942)
XLA Ops:
  0.0 21.6 %shard_map.64 = bf16[512,1024]{1,0:T(8,128)(2,1)S(1)} custom-call(bf16[512,2048]{1,0:T(8,128)(2,1)} %bitcast.6, bf16[2048,2,512]{2,1,0:T(2,128)(2,1)} %w_hbm.1, f32[1,512]{1,0:T(1,128)} %bitcast.8, f32[1,512]{1,0:T(1,128)} %bitcast.9, bf16[2,512,2048]{2,1,0:T(8,128)(2,1)} %r_hbm.1, f32[1,1024]{1,0:T(1,128)} %bitcast.7), custom_call_target="tpu_custom_call" | custom-call | tf_op jit(solution)/shard_map/pallas_call | solution.py:341
  21.6 1.0 %copy.8 = bf16[4,128,1024]{2,1,0:T(8,128)(2,1)} copy(bf16[4,128,1024]{2,1,0:T(8,128)(2,1)S(1)} %bitcast.5) | data formatting | bytes 2097152
